TPU v7x, 768 devices: a whole 4x8x12 slice. The times are simulated.
768 devices in a mesh: space: 96 (over z, x, core), member: 8 (over y).
Axes of the slice: x: 4, y: 8, z: 12, core: 2. Of those that a mesh axis runs over, the one named last changes fastest.
Arguments:
- coarse_vertex_embedding: bfloat16 [8, 3072, 1024], P('member', 'space'), may hold values from -6 to 6
- lattice_bypass_embedding: bfloat16 [8, 12288, 1024], P('member', 'space'), may hold values from -6 to 6
- initial_condition: float32 [8, 12288, 100], P('member', 'space'), may hold values from -6 to 6
- verifying_analysis: float32 [12288, 100], P('space'), may hold values from -8 to 8
- edge_index: int32 [12288, 3], P('space'), may hold values from 0 to 95
- area_weight: float32 [12288], P('space'), may hold values from 0.4 to 4
- variable_weight: float32 [100], replicated, may hold values from 0.2 to 2
- query_weight: bfloat16 [1024, 1024], replicated, may hold values from -2 to 2
- keyval_weight: bfloat16 [1024, 2048], replicated, may hold values from -0.1875 to 0.1875
- output_weight: bfloat16 [1024, 1024], replicated, may hold values from -0.1875 to 0.1875
- output_channel_matrix: bfloat16 [1024, 100], replicated, may hold values from -0.1875 to 0.1875
Outputs:
- grad_mesh: bfloat16 [8, 3072, 1024], P('member', 'space')
- grad_grid: bfloat16 [8, 12288, 1024], P('member', 'space')
- probabilistic_penalty: float32 [12288, 100], P(('space', 'member'))
Inputs may be any that keep to these rules, and one draw needn't show every extreme that they name: `edge_index`: node numbers 0 to 31 name nodes of the previous longitude sector, the next 32 the grid point's own sector, the last 32 the following sector; sectors wrap around the globe.
All inputs are finite; a program needn't handle non-finite values.
Results may differ from a plain program's by a relative error of at most 0.03.
Values may be sent and summed in bfloat16 or wider, within the bound.
No kernel may reach another device: no remote copies, remote signals or barrier semaphores. Data moves between devices by JAX's collectives and lax.ppermute only.
A program may use at most 64 MiB of HBM per device.

v0:
```python
import jax
import jax.numpy as jnp
from jax import lax
from jax.experimental import pallas as pl
from jax.experimental.pallas import tpu as pltpu
from jax.sharding import PartitionSpec as P

HEADS = 16
PAIRS = HEADS // 2
SOFT_CAP = 30.0
SOFTENED_QUAD = 0.01
FAIR_ALPHA = 0.95
OBJECTIVE_WEIGHT = 64.0
ROWS = 112
CHUNK = 512

F32 = jnp.float32
BF16 = jnp.bfloat16
MIB = 1024 * 1024

NN = (((1,), (0,)), ((), ()))
NT = (((1,), (1,)), ((), ()))
TN = (((0,), (0,)), ((), ()))


def mm(a, b, dims=NN):
    return lax.dot_general(a, b, dims, preferred_element_type=F32)


def split(x):
    hi = x.astype(BF16)
    return hi, (x - hi.astype(F32)).astype(BF16)


def diagonal(top, bottom):
    zero = jnp.zeros_like(top)
    return jnp.concatenate(
        [jnp.concatenate([top, zero], 1), jnp.concatenate([zero, bottom], 1)], 0
    )


def quadrants(full):
    return jnp.concatenate([full[:64, :128], full[64:, 128:]], 0)


def lanes_kernel(keep):
    first = (lax.broadcasted_iota(jnp.int32, (128, 128), 1) < 64).astype(F32)
    keep[:128] = first.astype(BF16)
    keep[128:] = (1.0 - first).astype(BF16)


def prepare_kernel(
    lattice, query_weight, channels_t, condition_t, query, query_hi, query_lo, base_t
):
    rows = lattice[...]
    for c in range(query_weight.shape[1] // CHUNK):
        at = slice(CHUNK * c, CHUNK * c + CHUNK)
        q = mm(rows, query_weight[:, at])
        query[:, at] = q.astype(BF16)
        hi, lo = split(q.T)
        query_hi[at, :] = hi
        query_lo[at, :] = lo
    variables = channels_t.shape[0]
    base_t[...] = jnp.zeros_like(base_t)
    base_t[:variables] = condition_t[:, 0, :] + mm(channels_t[...], rows, NT)


def attend_kernel(
    info, beside_late, across, beside_early, own, keyval_weight, query, query_hi, query_lo, edges_t, keep, area,
    variable,
    keyval, weight, weight_16, slant, mixture_t, query_halves, scale_t,
    nodes, score,
):
    block = own.shape[0]
    odd = info[1]
    nodes[block : 2 * block] = own[...]
    nodes[pl.ds(pl.multiple_of(odd * 2 * block, block), block)] = across[...]
    nodes[pl.ds(pl.multiple_of((1 - odd) * 2 * block, block), block)] = (
        beside_early[...] + beside_late[...]
    )
    slots, channels = nodes.shape
    points = edges_t.shape[1]
    x = nodes[...]
    for c in range(2 * channels // CHUNK):
        at = slice(CHUNK * c, CHUNK * c + CHUNK)
        keyval[:, at] = mm(x, keyval_weight[:, at]).astype(BF16)
    for p in range(PAIRS):
        at = slice(128 * p, 128 * p + 128)
        k = keyval[:, at]
        q_hi = query_hi[at, :]
        q_lo = query_lo[at, :]
        score[p] = mm(
            jnp.concatenate([k, k], 1),
            jnp.concatenate([diagonal(q_hi[:64], q_hi[64:]), diagonal(q_lo[:64], q_lo[64:])], 0),
        )
    number = lax.broadcasted_iota(jnp.int32, (slots, points), 0)
    count = jnp.zeros((slots, points), F32)
    for e in range(edges_t.shape[0]):
        count = count + (number == edges_t[e : e + 1, :]).astype(F32)
    count = jnp.concatenate([count, count], 1)
    for p in range(PAIRS):
        bent = jnp.tanh(score[p] * (1.0 / (8.0 * SOFT_CAP)))
        exponent = jnp.exp(SOFT_CAP * bent) * count
        w = exponent * (1.0 / jnp.sum(exponent, axis=0, keepdims=True))
        weight[p] = w
        weight_16[p] = w.astype(BF16)
        slant[p] = w * ((1.0 - bent * bent) * 0.125)
    left = keep[:128]
    right = keep[128:]
    for p in range(PAIRS):
        at = slice(128 * p, 128 * p + 128)
        v = keyval[:, channels + 128 * p : channels + 128 * p + 128]
        mixture_t[at, :] = quadrants(mm(v, weight_16[p], TN)).astype(BF16)
        query_halves[p] = jnp.concatenate([query[:, at] * left, query[:, at] * right], 0)
    variables = variable.shape[1]
    spread = jnp.concatenate(
        [
            jnp.broadcast_to(variable[...], (128, variables)),
            jnp.zeros((128, 128 - variables), F32),
        ],
        1,
    )
    scale_t[...] = spread.T[:ROWS] * area[...]


def joint_kernel(output_weight, channels_t, joint_t):
    variables, channels = channels_t.shape
    both = mm(channels_t[...], output_weight[...], NT)
    hi, lo = split(jnp.concatenate([both, jnp.zeros((ROWS - variables, channels), F32)], 0))
    joint_t[:ROWS] = hi
    joint_t[ROWS:] = lo


def forecast_kernel(joint_t, base_t, mixture_t, keyval, keep, piled, mine, value_joint):
    channels = mixture_t.shape[0]
    parts = mm(joint_t[...], mixture_t[...])
    forecast = (base_t[...] + (parts[:ROWS] + parts[ROWS:])).astype(BF16)
    mine[...] = forecast
    for m in range(piled.shape[0]):
        piled[m] = forecast
    slots = keyval.shape[0]
    pad = jnp.zeros((slots, 128 - ROWS), BF16)
    for p in range(PAIRS):
        at = slice(128 * p, 128 * p + 128)
        v = keyval[:, channels + 128 * p : channels + 128 * p + 128]
        hi = joint_t[:ROWS, at]
        lo = joint_t[ROWS:, at]
        for half in range(2):
            side = keep[128 * half : 128 * half + ROWS]
            high, low = split(
                mm(
                    jnp.concatenate([v, v], 1),
                    jnp.concatenate([hi * side, lo * side], 1),
                    NT,
                )
            )
            rows = slice((2 * p + half) * slots, (2 * p + half + 1) * slots)
            value_joint[rows, :] = jnp.concatenate([high, pad, low, pad], 1)


def backward_kernel(
    info, piled, mine, analysis_t, scale_t, joint_t, query_halves, value_joint, weight, weight_16,
    slant, keyval_weight, keep,
    term_across, term_beside, term_own, grad_score, slope,
    partial, slope_t, truth, terms, grad_weight,
):
    members = piled.shape[0]
    fair_eps = (1.0 - FAIR_ALPHA) / members
    variables = analysis_t.shape[0]
    truth[...] = jnp.zeros_like(truth)
    truth[:variables] = analysis_t[...]

    def bend(d):
        return d * lax.rsqrt(d * d + SOFTENED_QUAD)

    slope_t[ROWS:] = jnp.zeros((128 - ROWS, slope_t.shape[1]), F32)
    for r in range(0, ROWS, 16):
        at = slice(r, r + 16)
        forecast = mine[at].astype(F32)
        spread = jnp.zeros_like(forecast)
        for k in range(members):
            spread = spread + bend(forecast - piled[k, at].astype(F32))
        slope_t[at] = (OBJECTIVE_WEIGHT * scale_t[at]) * (
            bend(forecast - truth[at]) * (1.0 / members)
            - ((1.0 - fair_eps) / (members * (members - 1))) * spread
        )
    s_t = slope_t[...]
    s = s_t.T.astype(BF16)
    s_t = s_t.astype(BF16)
    slope[...] = s
    channels = keyval_weight.shape[1] // 2
    slots = partial.shape[0]
    grad_weight[...] = mm(value_joint[...], jnp.concatenate([s_t, s_t], 0))
    left = keep[:128]
    right = keep[128:]
    gm = mm(s[:, :ROWS], joint_t[:ROWS]).astype(BF16)
    for p in range(PAIRS):
        at = slice(128 * p, 128 * p + 128)
        v_at = slice(channels + 128 * p, channels + 128 * p + 128)
        halves = jnp.concatenate([gm[:, at] * left, gm[:, at] * right], 0)
        partial[:, v_at] = mm(weight_16[p], halves).astype(BF16)
    for p in range(PAIRS):
        low = 2 * p * slots
        gw = jnp.concatenate(
            [grad_weight[low : low + slots], grad_weight[low + slots : low + 2 * slots]], 1
        )
        w = weight[p]
        grad_score[p] = (
            slant[p] * (gw - jnp.sum(w * gw, axis=0, keepdims=True))
        ).astype(BF16)
    for p in range(PAIRS):
        at = slice(128 * p, 128 * p + 128)
        partial[:, at] = mm(grad_score[p], query_halves[p]).astype(BF16)
    terms[...] = (
        mm(partial[:, channels:], keyval_weight[:, channels:], NT)
        + mm(partial[:, :channels], keyval_weight[:, :channels], NT)
    ).astype(BF16)
    block = term_own.shape[0]
    odd = info[1]
    term_own[...] = terms[block : 2 * block]
    term_across[...] = terms[pl.ds(pl.multiple_of(odd * 2 * block, block), block)]
    term_beside[...] = terms[pl.ds(pl.multiple_of((1 - odd) * 2 * block, block), block)]


def finish_kernel(
    info, keyval, grad_score, query_weight, slope, channels_t, piled, analysis_t, scale_t,
    term_own, from_beside,
    grad_grid, penalty, total,
    grad_query, truth, turned,
):
    total[...] = term_own[...].astype(F32) + from_beside[...].astype(F32)
    variables = channels_t.shape[0]
    for p in range(PAIRS):
        at = slice(128 * p, 128 * p + 128)
        grad_query[:, at] = quadrants(mm(keyval[:, at], grad_score[p], TN)).T.astype(BF16)
    hidden = mm(slope[:, :variables], channels_t[...])
    for c in range(query_weight.shape[0] // CHUNK):
        at = slice(CHUNK * c, CHUNK * c + CHUNK)
        grad_grid[:, at] = (
            mm(grad_query[...], query_weight[at, :], NT) + hidden[:, at]
        ).astype(BF16)
    members = piled.shape[0]
    fair_eps = (1.0 - FAIR_ALPHA) / members
    truth[...] = jnp.zeros_like(truth)
    truth[:variables] = analysis_t[...]

    def soft(d):
        square = d * d + SOFTENED_QUAD
        return square * lax.rsqrt(square)

    turned[ROWS:] = jnp.zeros((128 - ROWS, 128), F32)
    for r in range(0, ROWS, 16):
        at = slice(r, r + 16)
        casts = [piled[m, at].astype(F32) for m in range(members)]
        goal = truth[at]
        accuracy = jnp.zeros_like(goal)
        spread = jnp.zeros_like(goal)
        for a in range(members):
            accuracy = accuracy + soft(casts[a] - goal)
            for b in range(a + 1, members):
                spread = spread + soft(casts[a] - casts[b])
        turned[at] = scale_t[at] * (
            accuracy * (1.0 / members) - ((1.0 - fair_eps) / (members * (members - 1))) * spread
        )
    turned[...] = turned[...].T
    rows = penalty.shape[0]
    start = pl.multiple_of(info[0] * rows, rows)
    penalty[...] = turned[pl.ds(start, rows), :variables]


def shaped(*dims, dtype=BF16):
    return jax.ShapeDtypeStruct(dims, dtype)


VMEM = pl.BlockSpec(memory_space=pltpu.VMEM)
HBM = pl.BlockSpec(memory_space=pltpu.HBM)
SMEM = pl.BlockSpec(memory_space=pltpu.SMEM)


def call(kernel, outs, scratch, args, limit, flops, moved, specs):
    specs = list(specs) + [VMEM] * (len(args) - len(specs))
    return pl.pallas_call(
        kernel,
        out_shape=outs,
        in_specs=specs,
        out_specs=[VMEM] * len(outs),
        scratch_shapes=scratch,
        compiler_params=pltpu.CompilerParams(vmem_limit_bytes=limit * MIB),
        cost_estimate=pl.CostEstimate(flops=flops, bytes_accessed=moved, transcendentals=0),
    )(*args)


def swap_across(value):
    count = lax.axis_size("space")
    return lax.ppermute(
        value, "space", [(i, (i + 1) % count if i % 2 else (i - 1) % count) for i in range(count)]
    )


def swap_beside(value, part=None):
    count = lax.axis_size("space")
    half = count // 4 * 2
    chosen = {None: range(count), 0: range(half), 1: range(half, count)}[part]
    return lax.ppermute(value, "space", [(i, i ^ 1) for i in chosen])


def per_device(
    coarse_vertex_embedding,
    lattice_bypass_embedding,
    initial_condition,
    verifying_analysis,
    edge_index,
    area_weight,
    variable_weight,
    query_weight,
    keyval_weight,
    output_weight,
    output_channel_matrix,
):
    own = coarse_vertex_embedding[0]
    lattice = lattice_bypass_embedding[0]
    block, channels = own.shape
    points = lattice.shape[0]
    variables = variable_weight.shape[0]
    slots = 3 * block
    members = lax.axis_size("member")
    condition_t = jnp.transpose(initial_condition, (2, 0, 1))
    analysis_t = verifying_analysis.T
    edges_t = edge_index.T
    channels_t = output_channel_matrix.T
    info = jnp.stack([lax.axis_index("member"), lax.axis_index("space") % 2]).astype(jnp.int32)

    beside_early = swap_beside(own, 0)
    across = swap_across(own)
    (keep,) = call(lanes_kernel, [shaped(256, 128)], [], (), 1, 3_000_000_000, 12_000_000, [])
    own, keep = lax.optimization_barrier((own, keep))
    beside_late = swap_beside(own, 1)
    query, query_hi, query_lo, base_t = call(
        prepare_kernel,
        [
            shaped(points, channels),
            shaped(channels, points),
            shaped(channels, points),
            shaped(ROWS, points, dtype=F32),
        ],
        [],
        (lattice, query_weight, channels_t, condition_t),
        4,
        1_000_000,
        1_000_000,
        [],
    )
    (joint_t,) = call(
        joint_kernel,
        [shaped(2 * ROWS, channels)],
        [],
        (output_weight, channels_t),
        4,
        3_000_000_000,
        10_000_000,
        [],
    )
    keyval, weight, weight_16, slant, mixture_t, query_halves, scale_t = call(
        attend_kernel,
        [
            shaped(slots, 2 * channels),
            shaped(PAIRS, slots, 2 * points, dtype=F32),
            shaped(PAIRS, slots, 2 * points),
            shaped(PAIRS, slots, 2 * points, dtype=F32),
            shaped(channels, points),
            shaped(PAIRS, 256, 128),
            shaped(ROWS, points, dtype=F32),
        ],
        [
            pltpu.VMEM((slots, channels), BF16),
            pltpu.VMEM((PAIRS, slots, 2 * points), F32),
        ],
        (
            info, beside_late, across, beside_early, own, keyval_weight, query, query_hi, query_lo, edges_t, keep,
            area_weight[None], variable_weight[None],
        ),
        4,
        2_000_000_000,
        8_000_000,
        [SMEM],
    )
    piled, mine, value_joint = call(
        forecast_kernel,
        [
            shaped(members, ROWS, points),
            shaped(ROWS, points),
            shaped(HEADS * slots, 256),
        ],
        [],
        (joint_t, base_t, mixture_t, keyval, keep),
        4,
        500_000_000,
        4_000_000,
        [],
    )
    piled = lax.all_to_all(piled, "member", split_axis=0, concat_axis=0, tiled=True)
    term_across, term_beside, term_own, grad_score, slope = call(
        backward_kernel,
        [
            shaped(block, channels),
            shaped(block, channels),
            shaped(block, channels),
            shaped(PAIRS, slots, 2 * points),
            shaped(points, 128),
        ],
        [
            pltpu.VMEM((slots, 2 * channels), BF16),
            pltpu.VMEM((128, points), F32),
            pltpu.VMEM((ROWS, points), F32),
            pltpu.VMEM((slots, channels), BF16),
            pltpu.VMEM((HEADS * slots, points), F32),
        ],
        (
            info, piled, mine, analysis_t, scale_t, joint_t, query_halves, value_joint, weight,
            weight_16, slant, keyval_weight, keep,
        ),
        6,
        1_500_000_000,
        8_000_000,
        [SMEM],
    )
    from_beside = swap_beside(term_beside)
    from_across = swap_across(term_across)
    grad_grid, penalty, total = call(
        finish_kernel,
        [
            shaped(points, channels),
            shaped(points // members, variables, dtype=F32),
            shaped(block, channels, dtype=F32),
        ],
        [
            pltpu.VMEM((points, channels), BF16),
            pltpu.VMEM((ROWS, points), F32),
            pltpu.VMEM((128, 128), F32),
        ],
        (
            info, keyval, grad_score, query_weight, slope, channels_t, piled, analysis_t, scale_t,
            term_own, from_beside,
        ),
        4,
        400_000_000,
        4_000_000,
        [SMEM],
    )
    grad_nodes = total + from_across.astype(F32)
    return (grad_nodes.astype(BF16)[None], grad_grid[None], penalty)


def solution(mesh):
    return jax.shard_map(
        per_device,
        mesh=mesh,
        in_specs=(
            P("member", "space", None),
            P("member", "space", None),
            P("member", "space", None),
            P("space", None),
            P("space", None),
            P("space"),
            P(),
            P(),
            P(),
            P(),
            P(),
        ),
        out_specs=(
            P("member", "space", None),
            P("member", "space", None),
            P(("space", "member"), None),
        ),
        check_vma=False,
    )
```

profile of v0, /device:TPU:8, one launch (start us, length us, event | category | flops | bytes accessed | tf_op | source)
XLA Modules:
  0.0 54.0 jit_solution(601487728470643911)
XLA Ops:
  0.6 0.0 copy-start.7
  0.6 0.0 copy-start.2
  0.7 0.0 copy-start.6
  0.7 2.1 %collective-permute-start.2 = (bf16[32,1024]{1,0:T(8,128)(2,1)}, bf16[32,1024]{1,0:T(8,128)(2,1)S(1)}, u32[]{:S(2)}, u32[]{:S(2)}) collective-permute-start(bf16[32,1024]{1,0:T(8,128)(2,1)} %bitcast.20), channel_id=1, source_target_pairs={{0,8},{8,0},{16,24},{24,16},{32,40},{40,32},{48,56},{56,48},{64,72... | collective-permute-start | bytes 196616 | tf_op jit(solution)/shard_map/ppermute | solution.py:304
  2.7 15.0 %collective-permute-start.1 = (bf16[32,1024]{1,0:T(8,128)(2,1)}, bf16[32,1024]{1,0:T(8,128)(2,1)S(1)}, u32[]{:S(2)}, u32[]{:S(2)}) collective-permute-start(bf16[32,1024]{1,0:T(8,128)(2,1)} %bitcast.21), channel_id=1, source_target_pairs={{0,760},{8,16},{16,8},{24,32},{32,24},{40,48},{48,40},{56,64},{64,... | collective-permute-start | bytes 196616 | tf_op jit(solution)/shard_map/ppermute | solution.py:295
  17.7 0.0 copy-done.7
  17.7 0.7 %collective-permute-start = (bf16[32,1024]{1,0:T(8,128)(2,1)S(1)}, bf16[32,1024]{1,0:T(8,128)(2,1)S(1)}, u32[]{:S(2)}, u32[]{:S(2)}) collective-permute-start(bf16[32,1024]{1,0:T(8,128)(2,1)S(1)} %bitcast.22), channel_id=1, source_target_pairs={{384,392},{392,384},{400,408},{408,400},{416,424},{424,416},{432,4... | collective-permute-start | bytes 196616 | tf_op jit(solution)/shard_map/ppermute | solution.py:304
  18.4 0.0 copy-done.2
  18.4 0.0 copy-done.6
  18.4 0.0 copy-start
  18.4 0.0 copy-start.3
  18.5 0.0 copy-start.5
  18.5 0.0 copy-start.1
  18.5 0.8 %shard_map.133.joint_t = bf16[224,1024]{1,0:T(8,128)(2,1)S(1)} custom-call(bf16[1024,1024]{1,0:T(8,128)(2,1)S(1)} %copy-done.6, bf16[100,1024]{1,0:T(8,128)(2,1)S(1)} %bitcast.13), custom_call_target="tpu_custom_call" | custom-call | flops 3000000000 | bytes 10000000 | tf_op jit(solution)/shard_map/pallas_call | solution.py:282
  19.3 0.0 copy-start.8
  19.3 0.0 copy-start.9
  19.3 0.0 copy-start.10
  19.3 0.7 %copy-done = bf16[1024,1024]{1,0:T(8,128)(2,1)S(1)} copy-done((bf16[1024,1024]{1,0:T(8,128)(2,1)S(1)}, bf16[1024,1024]{1,0:T(8,128)(2,1)}, u32[]{:S(2)}) %copy-start) | copy-done | bytes 2097176
  20.0 0.0 copy-done.3
  20.0 0.0 copy-done.5
  20.0 0.6 %shard_map.131 = (bf16[128,1024]{1,0:T(8,128)(2,1)S(1)}, bf16[1024,128]{1,0:T(8,128)(2,1)S(1)}, bf16[1024,128]{1,0:T(8,128)(2,1)S(1)}, f32[112,128]{1,0:T(8,128)S(1)}) custom-call(bf16[128,1024]{1,0:T(8,128)(2,1)S(1)} %bitcast.16, bf16[1024,1024]{1,0:T(8,128)(2,1)S(1)} %copy-done, bf16[100,1024]{1,0:T(8,128)(2,1)S(1)} %bitcast.14, f32[100,1,128]{2,1,0:T(1,128)S(1)} %bitcast.19), custom_call_target="tpu_custom_call" | custom-call | flops 1000000 | bytes 1000000 | tf_op jit(solution)/shard_map/pallas_call | solution.py:282
  20.6 0.1 pad_add_fusion.info
  20.7 0.0 collective-permute-done.beside_late
  20.7 0.0 collective-permute-done.2.beside_early
  20.7 0.0 collective-permute-done.1.across
  20.7 0.7 %copy-done.1 = bf16[1024,2048]{1,0:T(8,128)(2,1)S(1)} copy-done((bf16[1024,2048]{1,0:T(8,128)(2,1)S(1)}, bf16[1024,2048]{1,0:T(8,128)(2,1)}, u32[]{:S(2)}) %copy-start.1) | copy-done | bytes 4194328
  21.4 0.0 copy-done.8
  21.4 0.0 copy-done.9
  21.4 0.0 copy-done.10
  21.4 2.1 %shard_map.132 = (bf16[96,2048]{1,0:T(8,128)(2,1)S(1)}, f32[8,96,256]{2,1,0:T(8,128)S(1)}, bf16[8,96,256]{2,1,0:T(8,128)(2,1)S(1)}, f32[8,96,256]{2,1,0:T(8,128)...) custom-call(s32[2]{0:T(128)S(1)} %pad_add_fusion.info, ...), custom_call_target="tpu_custom_call" | custom-call | flops 2000000000 | bytes 8000000 | tf_op jit(solution)/shard_map/pallas_call | solution.py:282
  23.5 0.0 copy-start.4
  23.5 0.6 %shard_map.134 = (bf16[8,112,128]{2,1,0:T(8,128)(2,1)S(1)}, bf16[112,128]{1,0:T(8,128)(2,1)S(1)}, bf16[1536,256]{1,0:T(8,128)(2,1)S(1)}) custom-call(bf16[224,1024]{1,0:T(8,128)(2,1)S(1)} %shard_map.133.joint_t, f32[112,128]{1,0:T(8,128)S(1)} %get-tuple-element.33.base_t, bf16[1024,128]{1,0:T(8,128)(2,1)S(1)} %get-tuple-element.34.mixture_t, ...), custom_call_target="tpu_custom_call" | custom-call | flops 500000000 | bytes 4000000 | tf_op jit(solution)/shard_map/pallas_call | solution.py:282
  24.1 15.8 %all_to_all.5.piled = bf16[8,112,128]{2,1,0:T(8,128)(2,1)S(1)} all-to-all(bf16[8,112,128]{2,1,0:T(8,128)(2,1)S(1)} %get-tuple-element.35), channel_id=1, replica_groups=mesh['space'=96,'member'=8] {'member'}, dimensions={0} | all-to-all | bytes 458752 | tf_op jit(solution)/shard_map/all_to_all | solution.py:401
  39.8 0.0 copy-done.4
  39.8 2.6 %shard_map.135 = (bf16[32,1024]{1,0:T(8,128)(2,1)S(1)}, bf16[32,1024]{1,0:T(8,128)(2,1)S(1)}, bf16[32,1024]{1,0:T(8,128)(2,1)S(1)}, bf16[8,96,256]{2,1,0:T(8,128)(2,1)S(1)}, bf16[128,128]{1,0:T(8,128)(2,1)S(1)}) custom-call(s32[2]{0:T(128)S(1)} %pad_add_fusion.info, bf16[8,112,128]{2,1,0:T(8,128)(2,1)S(1)} %all_to_all.5.piled, ...), custom_call_target="tpu_custom_call" | custom-call | flops 1500000000 | bytes 8000000 | tf_op jit(solution)/shard_map/pallas_call | solution.py:282
  42.5 1.9 %collective-permute-start.3 = (bf16[32,1024]{1,0:T(8,128)(2,1)S(1)}, bf16[32,1024]{1,0:T(8,128)(2,1)S(1)}, u32[]{:S(2)}, u32[]{:S(2)}) collective-permute-start(bf16[32,1024]{1,0:T(8,128)(2,1)S(1)} %get-tuple-element.46), channel_id=1, source_target_pairs={{0,8},{8,0},{16,24},{24,16},{32,40},{40,32},{48,56},{56,48},{64,72... | collective-permute-start | bytes 196616 | tf_op jit(solution)/shard_map/ppermute | solution.py:304
  44.4 6.1 %collective-permute-start.4 = (bf16[32,1024]{1,0:T(8,128)(2,1)S(1)}, bf16[32,1024]{1,0:T(8,128)(2,1)S(1)}, u32[]{:S(2)}, u32[]{:S(2)}) collective-permute-start(bf16[32,1024]{1,0:T(8,128)(2,1)S(1)} %get-tuple-element.48), channel_id=1, source_target_pairs={{0,760},{8,16},{16,8},{24,32},{32,24},{40,48},{48,40},{56,64},{64,... | collective-permute-start | bytes 196616 | tf_op jit(solution)/shard_map/ppermute | solution.py:295
  50.6 0.0 collective-permute-done.3.from_beside
  50.6 2.6 %shard_map.136 = (bf16[128,1024]{1,0:T(8,128)(2,1)}, f32[16,100]{1,0:T(8,128)}, f32[32,1024]{1,0:T(8,128)S(1)}) custom-call(s32[2]{0:T(128)S(1)} %pad_add_fusion.info, bf16[96,2048]{1,0:T(8,128)(2,1)S(1)} %get-tuple-element.32.keyval, bf16[8,96,256]{2,1,0:T(8,128)(2,1)S(1)} %get-tuple-element.43.grad_score, bf16[1024,1024]{1,0:T(8,128)(2,1)S(1)} %copy-done, ...), custom_call_target="tpu_custom_call" | custom-call | flops 400000000 | bytes 4000000 | tf_op jit(solution)/shard_map/pallas_call | solution.py:282
  53.1 0.2 collective-permute-done.4
  53.3 0.7 %fusion = bf16[1,32,1024]{2,1,0:T(8,128)(2,1)} fusion(f32[32,1024]{1,0:T(8,128)S(1)} %get-tuple-element.47, bf16[32,1024]{1,0:T(8,128)(2,1)S(1)} %collective-permute-done.4), kind=kLoop, calls=%fused_computation.1 | loop fusion | flops 98304 | bytes 262144 | tf_op jit(solution)/shard_map/broadcast_in_dim | solution.py:451
  (1 shorter events, 0.0 us)
Async XLA Ops:
  0.6 17.1 %copy-start.7 = (bf16[1,32,1024]{2,1,0:T(8,128)(2,1)S(1)}, bf16[1,32,1024]{2,1,0:T(8,128)(2,1)}, u32[]{:S(2)}) copy-start(bf16[1,32,1024]{2,1,0:T(8,128)(2,1)} %param.11) | copy-start | bytes 196612
  0.6 17.8 %copy-start.2 = (bf16[1024,100]{0,1:T(8,128)(2,1)S(1)}, bf16[1024,100]{0,1:T(8,128)(2,1)}, u32[]{:S(2)}) copy-start(bf16[1024,100]{0,1:T(8,128)(2,1)} %param.21) | copy-start | bytes 614404
  0.7 17.8 %copy-start.6 = (bf16[1024,1024]{1,0:T(8,128)(2,1)S(1)}, bf16[1024,1024]{1,0:T(8,128)(2,1)}, u32[]{:S(2)}) copy-start(bf16[1024,1024]{1,0:T(8,128)(2,1)} %output_weight.1) | copy-start | bytes 6291460
  0.7 20.0 %collective-permute-start.2 = (bf16[32,1024]{1,0:T(8,128)(2,1)}, bf16[32,1024]{1,0:T(8,128)(2,1)S(1)}, u32[]{:S(2)}, u32[]{:S(2)}) collective-permute-start(bf16[32,1024]{1,0:T(8,128)(2,1)} %bitcast.20), channel_id=1, source_target_pairs={{0,8},{8,0},{16,24},{24,16},{32,40},{40,32},{48,56},{56,48},{64,72... | collective-permute-start | bytes 196616 | tf_op jit(solution)/shard_map/ppermute | solution.py:304
  2.7 18.0 %collective-permute-start.1 = (bf16[32,1024]{1,0:T(8,128)(2,1)}, bf16[32,1024]{1,0:T(8,128)(2,1)S(1)}, u32[]{:S(2)}, u32[]{:S(2)}) collective-permute-start(bf16[32,1024]{1,0:T(8,128)(2,1)} %bitcast.21), channel_id=1, source_target_pairs={{0,760},{8,16},{16,8},{24,32},{32,24},{40,48},{48,40},{56,64},{64,... | collective-permute-start | bytes 196616 | tf_op jit(solution)/shard_map/ppermute | solution.py:295
  17.7 3.0 %collective-permute-start = (bf16[32,1024]{1,0:T(8,128)(2,1)S(1)}, bf16[32,1024]{1,0:T(8,128)(2,1)S(1)}, u32[]{:S(2)}, u32[]{:S(2)}) collective-permute-start(bf16[32,1024]{1,0:T(8,128)(2,1)S(1)} %bitcast.22), channel_id=1, source_target_pairs={{384,392},{392,384},{400,408},{408,400},{416,424},{424,416},{432,4... | collective-permute-start | bytes 196616 | tf_op jit(solution)/shard_map/ppermute | solution.py:304
  18.4 1.6 %copy-start = (bf16[1024,1024]{1,0:T(8,128)(2,1)S(1)}, bf16[1024,1024]{1,0:T(8,128)(2,1)}, u32[]{:S(2)}) copy-start(bf16[1024,1024]{1,0:T(8,128)(2,1)} %query_weight.3) | copy-start | bytes 6291460
  18.4 1.6 %copy-start.3 = (bf16[1,128,1024]{2,1,0:T(8,128)(2,1)S(1)}, bf16[1,128,1024]{2,1,0:T(8,128)(2,1)}, u32[]{:S(2)}) copy-start(bf16[1,128,1024]{2,1,0:T(8,128)(2,1)} %param.12) | copy-start | bytes 786436
  18.5 1.6 %copy-start.5 = (f32[1,128,100]{1,0,2:T(1,128)S(1)}, f32[1,128,100]{1,0,2:T(1,128)}, u32[]{:S(2)}) copy-start(f32[1,128,100]{1,0,2:T(1,128)} %param.13) | copy-start | bytes 153604
  18.5 2.9 %copy-start.1 = (bf16[1024,2048]{1,0:T(8,128)(2,1)S(1)}, bf16[1024,2048]{1,0:T(8,128)(2,1)}, u32[]{:S(2)}) copy-start(bf16[1024,2048]{1,0:T(8,128)(2,1)} %keyval_weight.3) | copy-start | bytes 12582916
  19.3 2.1 %copy-start.8 = (s32[128,3]{0,1:T(4,128)S(1)}, s32[128,3]{0,1:T(4,128)}, u32[]{:S(2)}) copy-start(s32[128,3]{0,1:T(4,128)} %param.15) | copy-start | bytes 4612
  19.3 2.1 %copy-start.9 = (f32[128]{0:T(128)S(1)}, f32[128]{0:T(128)}, u32[]{:S(2)}) copy-start(f32[128]{0:T(128)} %param.16) | copy-start | bytes 1540
  19.3 2.1 %copy-start.10 = (f32[100]{0:T(128)S(1)}, f32[100]{0:T(128)}, u32[]{:S(2)}) copy-start(f32[100]{0:T(128)} %param.17) | copy-start | bytes 1204
  23.5 16.3 %copy-start.4 = (f32[128,100]{0,1:T(8,128)S(1)}, f32[128,100]{0,1:T(8,128)}, u32[]{:S(2)}) copy-start(f32[128,100]{0,1:T(8,128)} %param.14) | copy-start | bytes 153604
  42.5 8.1 %collective-permute-start.3 = (bf16[32,1024]{1,0:T(8,128)(2,1)S(1)}, bf16[32,1024]{1,0:T(8,128)(2,1)S(1)}, u32[]{:S(2)}, u32[]{:S(2)}) collective-permute-start(bf16[32,1024]{1,0:T(8,128)(2,1)S(1)} %get-tuple-element.46), channel_id=1, source_target_pairs={{0,8},{8,0},{16,24},{24,16},{32,40},{40,32},{48,56},{56,48},{64,72... | collective-permute-start | bytes 196616 | tf_op jit(solution)/shard_map/ppermute | solution.py:304
  44.4 8.9 %collective-permute-start.4 = (bf16[32,1024]{1,0:T(8,128)(2,1)S(1)}, bf16[32,1024]{1,0:T(8,128)(2,1)S(1)}, u32[]{:S(2)}, u32[]{:S(2)}) collective-permute-start(bf16[32,1024]{1,0:T(8,128)(2,1)S(1)} %get-tuple-element.48), channel_id=1, source_target_pairs={{0,760},{8,16},{16,8},{24,32},{32,24},{40,48},{48,40},{56,64},{64,... | collective-permute-start | bytes 196616 | tf_op jit(solution)/shard_map/ppermute | solution.py:295
where the time goes:
time: 54.3 us; the launch traced here: 54 us
  starting transfers between devices  25.7 us (47%)
  blocking collectives  15.8 us (29%)
  Pallas kernels  9.26 us (17%)
  local copies, waits for them, and re-layouts  1.44 us (3%)
  between operations  0.86 us (2%)
  other arithmetic  0.73 us (1%)
    ppermute x2, starting transfers between devices, swap_across(): lax.ppermute(value, 'space', [(i, (i + 1) % count if i % 2 else (i - 1) %...  21.1 us
    all_to_all x1, blocking collectives, per_device(): lax.all_to_all(piled, 'member', split_axis=0, concat_axis=0, tiled=True)  15.8 us
    pallas_call x7, Pallas kernels, call(): pl.pallas_call(kernel, out_shape=outs, in_specs=specs, out_specs=[VMEM] *...  9.26 us
    ppermute x3, starting transfers between devices, swap_beside(): return lax.ppermute(value, 'space', [(i, i ^ 1) for i in chosen])  4.64 us
    unnamed x22, local copies, waits for them, and re-layouts  1.44 us
  transfers between devices with their start and end apart: 5, of which 1 were waited for; matrix products, arithmetic and copies ran while one was open for 0% of the time, Pallas kernels for 7%

commit v1 on v0

--- a/solution.py
+++ b/solution.py
@@ -50,26 +50,39 @@
 
 
 def prepare_kernel(
-    lattice, query_weight, channels_t, condition_t, query, query_hi, query_lo, base_t
+    lattice, query_weight, channels_t, condition_t, keep, area, variable,
+    query_hi, query_lo, base_t, query_halves, scale_t,
 ):
     rows = lattice[...]
+    left = keep[:128]
+    right = keep[128:]
     for c in range(query_weight.shape[1] // CHUNK):
         at = slice(CHUNK * c, CHUNK * c + CHUNK)
         q = mm(rows, query_weight[:, at])
-        query[:, at] = q.astype(BF16)
         hi, lo = split(q.T)
         query_hi[at, :] = hi
         query_lo[at, :] = lo
+        rounded = q.astype(BF16)
+        for p in range(CHUNK // 128):
+            pair = rounded[:, 128 * p : 128 * p + 128]
+            query_halves[c * (CHUNK // 128) + p] = jnp.concatenate([pair * left, pair * right], 0)
     variables = channels_t.shape[0]
+    spread = jnp.concatenate(
+        [
+            jnp.broadcast_to(variable[...], (128, variables)),
+            jnp.zeros((128, 128 - variables), F32),
+        ],
+        1,
+    )
+    scale_t[...] = spread.T[:ROWS] * area[...]
     base_t[...] = jnp.zeros_like(base_t)
     base_t[:variables] = condition_t[:, 0, :] + mm(channels_t[...], rows, NT)
 
 
 def attend_kernel(
-    info, beside_late, across, beside_early, own, keyval_weight, query, query_hi, query_lo, edges_t, keep, area,
-    variable,
-    keyval, weight, weight_16, slant, mixture_t, query_halves, scale_t,
-    nodes, score,
+    info, beside_late, across, beside_early, own, keyval_weight, query_hi, query_lo, edges_t, keep, joint_t, base_t,
+    piled, mine, keyval, weight, weight_16, slant, value_joint,
+    nodes, score, mixture_t,
 ):
     block = own.shape[0]
     odd = info[1]
@@ -105,40 +118,15 @@
         weight[p] = w
         weight_16[p] = w.astype(BF16)
         slant[p] = w * ((1.0 - bent * bent) * 0.125)
-    left = keep[:128]
-    right = keep[128:]
     for p in range(PAIRS):
         at = slice(128 * p, 128 * p + 128)
         v = keyval[:, channels + 128 * p : channels + 128 * p + 128]
         mixture_t[at, :] = quadrants(mm(v, weight_16[p], TN)).astype(BF16)
-        query_halves[p] = jnp.concatenate([query[:, at] * left, query[:, at] * right], 0)
-    variables = variable.shape[1]
-    spread = jnp.concatenate(
-        [
-            jnp.broadcast_to(variable[...], (128, variables)),
-            jnp.zeros((128, 128 - variables), F32),
-        ],
-        1,
-    )
-    scale_t[...] = spread.T[:ROWS] * area[...]
-
-
-def joint_kernel(output_weight, channels_t, joint_t):
-    variables, channels = channels_t.shape
-    both = mm(channels_t[...], output_weight[...], NT)
-    hi, lo = split(jnp.concatenate([both, jnp.zeros((ROWS - variables, channels), F32)], 0))
-    joint_t[:ROWS] = hi
-    joint_t[ROWS:] = lo
-
-
-def forecast_kernel(joint_t, base_t, mixture_t, keyval, keep, piled, mine, value_joint):
-    channels = mixture_t.shape[0]
     parts = mm(joint_t[...], mixture_t[...])
     forecast = (base_t[...] + (parts[:ROWS] + parts[ROWS:])).astype(BF16)
     mine[...] = forecast
     for m in range(piled.shape[0]):
         piled[m] = forecast
-    slots = keyval.shape[0]
     pad = jnp.zeros((slots, 128 - ROWS), BF16)
     for p in range(PAIRS):
         at = slice(128 * p, 128 * p + 128)
@@ -156,6 +144,14 @@
             )
             rows = slice((2 * p + half) * slots, (2 * p + half + 1) * slots)
             value_joint[rows, :] = jnp.concatenate([high, pad, low, pad], 1)
+
+
+def joint_kernel(output_weight, channels_t, joint_t):
+    variables, channels = channels_t.shape
+    both = mm(channels_t[...], output_weight[...], NT)
+    hi, lo = split(jnp.concatenate([both, jnp.zeros((ROWS - variables, channels), F32)], 0))
+    joint_t[:ROWS] = hi
+    joint_t[ROWS:] = lo
 
 
 def backward_kernel(
@@ -297,10 +293,10 @@
     )
 
 
-def swap_beside(value, part=None):
+def swap_beside(value, part):
     count = lax.axis_size("space")
     half = count // 4 * 2
-    chosen = {None: range(count), 0: range(half), 1: range(half, count)}[part]
+    chosen = (range(half), range(half, count))[part]
     return lax.ppermute(value, "space", [(i, i ^ 1) for i in chosen])
 
 
@@ -335,16 +331,20 @@
     (keep,) = call(lanes_kernel, [shaped(256, 128)], [], (), 1, 3_000_000_000, 12_000_000, [])
     own, keep = lax.optimization_barrier((own, keep))
     beside_late = swap_beside(own, 1)
-    query, query_hi, query_lo, base_t = call(
+    query_hi, query_lo, base_t, query_halves, scale_t = call(
         prepare_kernel,
         [
-            shaped(points, channels),
             shaped(channels, points),
             shaped(channels, points),
             shaped(ROWS, points, dtype=F32),
+            shaped(PAIRS, 256, 128),
+            shaped(ROWS, points, dtype=F32),
         ],
         [],
-        (lattice, query_weight, channels_t, condition_t),
+        (
+            lattice, query_weight, channels_t, condition_t, keep, area_weight[None],
+            variable_weight[None],
+        ),
         4,
         1_000_000,
         1_000_000,
@@ -360,43 +360,30 @@
         10_000_000,
         [],
     )
-    keyval, weight, weight_16, slant, mixture_t, query_halves, scale_t = call(
+    piled, mine, keyval, weight, weight_16, slant, value_joint = call(
         attend_kernel,
         [
+            shaped(members, ROWS, points),
+            shaped(ROWS, points),
             shaped(slots, 2 * channels),
             shaped(PAIRS, slots, 2 * points, dtype=F32),
             shaped(PAIRS, slots, 2 * points),
             shaped(PAIRS, slots, 2 * points, dtype=F32),
-            shaped(channels, points),
-            shaped(PAIRS, 256, 128),
-            shaped(ROWS, points, dtype=F32),
+            shaped(HEADS * slots, 256),
         ],
         [
             pltpu.VMEM((slots, channels), BF16),
             pltpu.VMEM((PAIRS, slots, 2 * points), F32),
+            pltpu.VMEM((channels, points), BF16),
         ],
         (
-            info, beside_late, across, beside_early, own, keyval_weight, query, query_hi, query_lo, edges_t, keep,
-            area_weight[None], variable_weight[None],
+            info, beside_late, across, beside_early, own, keyval_weight, query_hi, query_lo,
+            edges_t, keep, joint_t, base_t,
         ),
         4,
         2_000_000_000,
         8_000_000,
         [SMEM],
-    )
-    piled, mine, value_joint = call(
-        forecast_kernel,
-        [
-            shaped(members, ROWS, points),
-            shaped(ROWS, points),
-            shaped(HEADS * slots, 256),
-        ],
-        [],
-        (joint_t, base_t, mixture_t, keyval, keep),
-        4,
-        500_000_000,
-        4_000_000,
-        [],
     )
     piled = lax.all_to_all(piled, "member", split_axis=0, concat_axis=0, tiled=True)
     term_across, term_beside, term_own, grad_score, slope = call(
@@ -424,7 +411,8 @@
         8_000_000,
         [SMEM],
     )
-    from_beside = swap_beside(term_beside)
+    from_beside = swap_beside(term_beside, 0)
+    from_late = swap_beside(term_beside, 1)
     from_across = swap_across(term_across)
     grad_grid, penalty, total = call(
         finish_kernel,
@@ -447,7 +435,7 @@
         4_000_000,
         [SMEM],
     )
-    grad_nodes = total + from_across.astype(F32)
+    grad_nodes = total + from_across.astype(F32) + from_late.astype(F32)
     return (grad_nodes.astype(BF16)[None], grad_grid[None], penalty)
 
 

time: 54.3 us -> 54.1 us (level)
  starting transfers between devices: 25.7 us -> 25.1 us
  waiting for transfers between devices: 0.19 us -> 0.78 us
    ppermute x2, starting transfers between devices: 21.1 us -> 19.8 us  [swap_across(): lax.ppermute(value, 'space', [(i, (i + 1) % count if i % 2 else (i - 1) %...]
    ppermute x3 -> x4, starting transfers between devices: 4.64 us -> 5.3 us  [swap_beside(): return lax.ppermute(value, 'space', [(i, i ^ 1) for i in chosen])]
    ppermute x2, waiting for transfers between devices: 0.18 us -> 0.77 us  [swap_across(): lax.ppermute(value, 'space', [(i, (i + 1) % count if i % 2 else (i - 1) %...]
    pallas_call x7 -> x6, Pallas kernels: 9.26 us -> 9.18 us  [call(): pl.pallas_call(kernel, out_shape=outs, in_specs=specs, out_specs=[VMEM] *...]
  transfers between devices with their start and end apart: 5 -> 6, of which waited for: 1 -> 1; matrix products, arithmetic and copies ran while one was open for 0% -> 0% of each run, Pallas kernels for 7% -> 7%
where the time goes in v1:
time: 54.1 us; the launch traced here: 53.9 us
  starting transfers between devices  25.1 us (46%)
  blocking collectives  15.8 us (29%)
  Pallas kernels  9.18 us (17%)
  local copies, waits for them, and re-layouts  1.41 us (3%)
  between operations  0.85 us (2%)
  waiting for transfers between devices  0.78 us (1%)
  other arithmetic  0.74 us (1%)
    ppermute x2, starting transfers between devices, swap_across(): lax.ppermute(value, 'space', [(i, (i + 1) % count if i % 2 else (i - 1) %...  19.8 us
    all_to_all x1, blocking collectives, per_device(): lax.all_to_all(piled, 'member', split_axis=0, concat_axis=0, tiled=True)  15.8 us
    pallas_call x6, Pallas kernels, call(): pl.pallas_call(kernel, out_shape=outs, in_specs=specs, out_specs=[VMEM] *...  9.18 us
    ppermute x4, starting transfers between devices, swap_beside(): return lax.ppermute(value, 'space', [(i, i ^ 1) for i in chosen])  5.3 us
    unnamed x22, local copies, waits for them, and re-layouts  1.41 us
  transfers between devices with their start and end apart: 6, of which 1 were waited for; matrix products, arithmetic and copies ran while one was open for 0% of the time, Pallas kernels for 7%

profile of v1, /device:TPU:8, one launch (start us, length us, event | category | flops | bytes accessed | tf_op | source)
XLA Modules:
  0.0 53.9 jit_solution(6110264543132317532)
XLA Ops:
  0.6 0.0 copy-start.9
  0.6 0.0 copy-start.2
  0.7 0.0 copy-start.8
  0.7 2.1 %collective-permute-start.2 = (bf16[32,1024]{1,0:T(8,128)(2,1)}, bf16[32,1024]{1,0:T(8,128)(2,1)S(1)}, u32[]{:S(2)}, u32[]{:S(2)}) collective-permute-start(bf16[32,1024]{1,0:T(8,128)(2,1)} %bitcast.22), channel_id=1, source_target_pairs={{0,8},{8,0},{16,24},{24,16},{32,40},{40,32},{48,56},{56,48},{64,72... | collective-permute-start | bytes 196616 | tf_op jit(solution)/shard_map/ppermute | solution.py:300
  2.7 15.0 %collective-permute-start.1 = (bf16[32,1024]{1,0:T(8,128)(2,1)}, bf16[32,1024]{1,0:T(8,128)(2,1)S(1)}, u32[]{:S(2)}, u32[]{:S(2)}) collective-permute-start(bf16[32,1024]{1,0:T(8,128)(2,1)} %bitcast.23), channel_id=1, source_target_pairs={{0,760},{8,16},{16,8},{24,32},{32,24},{40,48},{48,40},{56,64},{64,... | collective-permute-start | bytes 196616 | tf_op jit(solution)/shard_map/ppermute | solution.py:291
  17.7 0.0 copy-done.9
  17.7 0.7 %collective-permute-start = (bf16[32,1024]{1,0:T(8,128)(2,1)S(1)}, bf16[32,1024]{1,0:T(8,128)(2,1)S(1)}, u32[]{:S(2)}, u32[]{:S(2)}) collective-permute-start(bf16[32,1024]{1,0:T(8,128)(2,1)S(1)} %bitcast.24), channel_id=1, source_target_pairs={{384,392},{392,384},{400,408},{408,400},{416,424},{424,416},{432,4... | collective-permute-start | bytes 196616 | tf_op jit(solution)/shard_map/ppermute | solution.py:300
  18.4 0.0 copy-done.2
  18.4 0.0 copy-done.8
  18.4 0.0 copy-start
  18.4 0.0 copy-start.3
  18.5 0.0 copy-start.5
  18.5 0.0 copy-start.6
  18.5 0.0 copy-start.7
  18.5 0.0 copy-start.1
  18.5 0.8 %shard_map.132.joint_t = bf16[224,1024]{1,0:T(8,128)(2,1)S(1)} custom-call(bf16[1024,1024]{1,0:T(8,128)(2,1)S(1)} %copy-done.8, bf16[100,1024]{1,0:T(8,128)(2,1)S(1)} %bitcast.13), custom_call_target="tpu_custom_call" | custom-call | flops 3000000000 | bytes 10000000 | tf_op jit(solution)/shard_map/pallas_call | solution.py:278
  19.3 0.0 copy-start.10
  19.3 0.7 %copy-done = bf16[1024,1024]{1,0:T(8,128)(2,1)S(1)} copy-done((bf16[1024,1024]{1,0:T(8,128)(2,1)S(1)}, bf16[1024,1024]{1,0:T(8,128)(2,1)}, u32[]{:S(2)}) %copy-start) | copy-done | bytes 2097176
  20.0 0.0 copy-done.3
  20.0 0.0 copy-done.5
  20.0 0.0 copy-done.6
  20.0 0.0 copy-done.7
  20.0 0.6 %shard_map.131 = (bf16[1024,128]{1,0:T(8,128)(2,1)S(1)}, bf16[1024,128]{1,0:T(8,128)(2,1)S(1)}, f32[112,128]{1,0:T(8,128)S(1)}, bf16[8,256,128]{2,1,0:T(8,128)(2,1)S(1)}, f32[112,128]{1,0:T(8,128)S(1)}) custom-call(bf16[128,1024]{1,0:T(8,128)(2,1)S(1)} %bitcast.16, bf16[1024,1024]{1,0:T(8,128)(2,1)S(1)} %copy-done, bf16[100,1024]{1,0:T(8,128)(2,1)S(1)} %bitcast.14, ...), custom_call_target="tpu_custom_call" | custom-call | flops 1000000 | bytes 1000000 | tf_op jit(solution)/shard_map/pallas_call | solution.py:278
  20.7 0.1 pad_add_fusion.info
  20.7 0.0 collective-permute-done.beside_late
  20.7 0.0 collective-permute-done.2.beside_early
  20.7 0.0 collective-permute-done.1.across
  20.7 0.7 %copy-done.1 = bf16[1024,2048]{1,0:T(8,128)(2,1)S(1)} copy-done((bf16[1024,2048]{1,0:T(8,128)(2,1)S(1)}, bf16[1024,2048]{1,0:T(8,128)(2,1)}, u32[]{:S(2)}) %copy-start.1) | copy-done | bytes 4194328
  21.4 0.0 copy-done.10
  21.4 0.0 copy-start.4
  21.4 2.5 %shard_map.133 = (bf16[8,112,128]{2,1,0:T(8,128)(2,1)S(1)}, bf16[112,128]{1,0:T(8,128)(2,1)S(1)}, bf16[96,2048]{1,0:T(8,128)(2,1)S(1)}, f32[8,96,256]{2,1,0:T(8,...) custom-call(s32[2]{0:T(128)S(1)} %pad_add_fusion.info, ...), custom_call_target="tpu_custom_call" | custom-call | flops 2000000000 | bytes 8000000 | tf_op jit(solution)/shard_map/pallas_call | solution.py:278
  23.9 15.8 %all_to_all.5.piled = bf16[8,112,128]{2,1,0:T(8,128)(2,1)S(1)} all-to-all(bf16[8,112,128]{2,1,0:T(8,128)(2,1)S(1)} %get-tuple-element.31), channel_id=1, replica_groups=mesh['space'=96,'member'=8] {'member'}, dimensions={0} | all-to-all | bytes 458752 | tf_op jit(solution)/shard_map/all_to_all | solution.py:388
  39.7 0.0 copy-done.4
  39.7 2.6 %shard_map.134 = (bf16[32,1024]{1,0:T(8,128)(2,1)S(1)}, bf16[32,1024]{1,0:T(8,128)(2,1)S(1)}, bf16[32,1024]{1,0:T(8,128)(2,1)S(1)}, bf16[8,96,256]{2,1,0:T(8,128)(2,1)S(1)}, bf16[128,128]{1,0:T(8,128)(2,1)S(1)}) custom-call(s32[2]{0:T(128)S(1)} %pad_add_fusion.info, bf16[8,112,128]{2,1,0:T(8,128)(2,1)S(1)} %all_to_all.5.piled, ...), custom_call_target="tpu_custom_call" | custom-call | flops 1500000000 | bytes 8000000 | tf_op jit(solution)/shard_map/pallas_call | solution.py:278
  42.4 1.9 %collective-permute-start.3 = (bf16[32,1024]{1,0:T(8,128)(2,1)S(1)}, bf16[32,1024]{1,0:T(8,128)(2,1)S(1)}, u32[]{:S(2)}, u32[]{:S(2)}) collective-permute-start(bf16[32,1024]{1,0:T(8,128)(2,1)S(1)} %get-tuple-element.42), channel_id=1, source_target_pairs={{0,8},{8,0},{16,24},{24,16},{32,40},{40,32},{48,56},{56,48},{64,72... | collective-permute-start | bytes 196616 | tf_op jit(solution)/shard_map/ppermute | solution.py:300
  44.3 4.9 %collective-permute-start.4 = (bf16[32,1024]{1,0:T(8,128)(2,1)S(1)}, bf16[32,1024]{1,0:T(8,128)(2,1)S(1)}, u32[]{:S(2)}, u32[]{:S(2)}) collective-permute-start(bf16[32,1024]{1,0:T(8,128)(2,1)S(1)} %get-tuple-element.44), channel_id=1, source_target_pairs={{0,760},{8,16},{16,8},{24,32},{32,24},{40,48},{48,40},{56,64},{64,... | collective-permute-start | bytes 196616 | tf_op jit(solution)/shard_map/ppermute | solution.py:291
  49.2 0.7 %collective-permute-start.5 = (bf16[32,1024]{1,0:T(8,128)(2,1)S(1)}, bf16[32,1024]{1,0:T(8,128)(2,1)S(1)}, u32[]{:S(2)}, u32[]{:S(2)}) collective-permute-start(bf16[32,1024]{1,0:T(8,128)(2,1)S(1)} %get-tuple-element.42), channel_id=1, source_target_pairs={{384,392},{392,384},{400,408},{408,400},{416,424},{424,416},{432,4... | collective-permute-start | bytes 196616 | tf_op jit(solution)/shard_map/ppermute | solution.py:300
  49.8 0.0 collective-permute-done.3.from_beside
  49.9 2.6 %shard_map.135 = (bf16[128,1024]{1,0:T(8,128)(2,1)}, f32[16,100]{1,0:T(8,128)}, f32[32,1024]{1,0:T(8,128)S(1)}) custom-call(s32[2]{0:T(128)S(1)} %pad_add_fusion.info, bf16[96,2048]{1,0:T(8,128)(2,1)S(1)} %get-tuple-element.30.keyval, bf16[8,96,256]{2,1,0:T(8,128)(2,1)S(1)} %get-tuple-element.39.grad_score, bf16[1024,1024]{1,0:T(8,128)(2,1)S(1)} %copy-done, ...), custom_call_target="tpu_custom_call" | custom-call | flops 400000000 | bytes 4000000 | tf_op jit(solution)/shard_map/pallas_call | solution.py:278
  52.4 0.8 %collective-permute-done.4 = bf16[32,1024]{1,0:T(8,128)(2,1)S(1)} collective-permute-done((bf16[32,1024]{1,0:T(8,128)(2,1)S(1)}, bf16[32,1024]{1,0:T(8,128)(2,1)S(1)}, u32[]{:S(2)}, u32[]{:S(2)}) %collective-permute-start.4) | collective-permute-done | bytes 65568 | tf_op jit(solution)/shard_map/ppermute | solution.py:291
  53.2 0.0 collective-permute-done.5
  53.2 0.7 %fusion = bf16[1,32,1024]{2,1,0:T(8,128)(2,1)} fusion(bf16[32,1024]{1,0:T(8,128)(2,1)S(1)} %collective-permute-done.5, f32[32,1024]{1,0:T(8,128)S(1)} %get-tuple-element.43, bf16[32,1024]{1,0:T(8,128)(2,1)S(1)} %collective-permute-done.4), kind=kLoop, calls=%fused_computation.1 | loop fusion | flops 163840 | bytes 327680 | tf_op jit(solution)/shard_map/broadcast_in_dim | solution.py:439
  (1 shorter events, 0.0 us)
Async XLA Ops:
  0.6 17.1 %copy-start.9 = (bf16[1,32,1024]{2,1,0:T(8,128)(2,1)S(1)}, bf16[1,32,1024]{2,1,0:T(8,128)(2,1)}, u32[]{:S(2)}) copy-start(bf16[1,32,1024]{2,1,0:T(8,128)(2,1)} %param.11) | copy-start | bytes 196612
  0.6 17.8 %copy-start.2 = (bf16[1024,100]{0,1:T(8,128)(2,1)S(1)}, bf16[1024,100]{0,1:T(8,128)(2,1)}, u32[]{:S(2)}) copy-start(bf16[1024,100]{0,1:T(8,128)(2,1)} %param.21) | copy-start | bytes 614404
  0.7 17.8 %copy-start.8 = (bf16[1024,1024]{1,0:T(8,128)(2,1)S(1)}, bf16[1024,1024]{1,0:T(8,128)(2,1)}, u32[]{:S(2)}) copy-start(bf16[1024,1024]{1,0:T(8,128)(2,1)} %output_weight.1) | copy-start | bytes 6291460
  0.7 20.1 %collective-permute-start.2 = (bf16[32,1024]{1,0:T(8,128)(2,1)}, bf16[32,1024]{1,0:T(8,128)(2,1)S(1)}, u32[]{:S(2)}, u32[]{:S(2)}) collective-permute-start(bf16[32,1024]{1,0:T(8,128)(2,1)} %bitcast.22), channel_id=1, source_target_pairs={{0,8},{8,0},{16,24},{24,16},{32,40},{40,32},{48,56},{56,48},{64,72... | collective-permute-start | bytes 196616 | tf_op jit(solution)/shard_map/ppermute | solution.py:300
  2.7 18.0 %collective-permute-start.1 = (bf16[32,1024]{1,0:T(8,128)(2,1)}, bf16[32,1024]{1,0:T(8,128)(2,1)S(1)}, u32[]{:S(2)}, u32[]{:S(2)}) collective-permute-start(bf16[32,1024]{1,0:T(8,128)(2,1)} %bitcast.23), channel_id=1, source_target_pairs={{0,760},{8,16},{16,8},{24,32},{32,24},{40,48},{48,40},{56,64},{64,... | collective-permute-start | bytes 196616 | tf_op jit(solution)/shard_map/ppermute | solution.py:291
  17.7 3.0 %collective-permute-start = (bf16[32,1024]{1,0:T(8,128)(2,1)S(1)}, bf16[32,1024]{1,0:T(8,128)(2,1)S(1)}, u32[]{:S(2)}, u32[]{:S(2)}) collective-permute-start(bf16[32,1024]{1,0:T(8,128)(2,1)S(1)} %bitcast.24), channel_id=1, source_target_pairs={{384,392},{392,384},{400,408},{408,400},{416,424},{424,416},{432,4... | collective-permute-start | bytes 196616 | tf_op jit(solution)/shard_map/ppermute | solution.py:300
  18.4 1.6 %copy-start = (bf16[1024,1024]{1,0:T(8,128)(2,1)S(1)}, bf16[1024,1024]{1,0:T(8,128)(2,1)}, u32[]{:S(2)}) copy-start(bf16[1024,1024]{1,0:T(8,128)(2,1)} %query_weight.3) | copy-start | bytes 6291460
  18.4 1.6 %copy-start.3 = (bf16[1,128,1024]{2,1,0:T(8,128)(2,1)S(1)}, bf16[1,128,1024]{2,1,0:T(8,128)(2,1)}, u32[]{:S(2)}) copy-start(bf16[1,128,1024]{2,1,0:T(8,128)(2,1)} %param.12) | copy-start | bytes 786436
  18.5 1.6 %copy-start.5 = (f32[1,128,100]{1,0,2:T(1,128)S(1)}, f32[1,128,100]{1,0,2:T(1,128)}, u32[]{:S(2)}) copy-start(f32[1,128,100]{1,0,2:T(1,128)} %param.13) | copy-start | bytes 153604
  18.5 1.6 %copy-start.6 = (f32[128]{0:T(128)S(1)}, f32[128]{0:T(128)}, u32[]{:S(2)}) copy-start(f32[128]{0:T(128)} %param.16) | copy-start | bytes 1540
  18.5 1.6 %copy-start.7 = (f32[100]{0:T(128)S(1)}, f32[100]{0:T(128)}, u32[]{:S(2)}) copy-start(f32[100]{0:T(128)} %param.17) | copy-start | bytes 1204
  18.5 2.9 %copy-start.1 = (bf16[1024,2048]{1,0:T(8,128)(2,1)S(1)}, bf16[1024,2048]{1,0:T(8,128)(2,1)}, u32[]{:S(2)}) copy-start(bf16[1024,2048]{1,0:T(8,128)(2,1)} %keyval_weight.3) | copy-start | bytes 12582916
  19.3 2.1 %copy-start.10 = (s32[128,3]{0,1:T(4,128)S(1)}, s32[128,3]{0,1:T(4,128)}, u32[]{:S(2)}) copy-start(s32[128,3]{0,1:T(4,128)} %param.15) | copy-start | bytes 4612
  21.4 18.3 %copy-start.4 = (f32[128,100]{0,1:T(8,128)S(1)}, f32[128,100]{0,1:T(8,128)}, u32[]{:S(2)}) copy-start(f32[128,100]{0,1:T(8,128)} %param.14) | copy-start | bytes 153604
  42.4 7.5 %collective-permute-start.3 = (bf16[32,1024]{1,0:T(8,128)(2,1)S(1)}, bf16[32,1024]{1,0:T(8,128)(2,1)S(1)}, u32[]{:S(2)}, u32[]{:S(2)}) collective-permute-start(bf16[32,1024]{1,0:T(8,128)(2,1)S(1)} %get-tuple-element.42), channel_id=1, source_target_pairs={{0,8},{8,0},{16,24},{24,16},{32,40},{40,32},{48,56},{56,48},{64,72... | collective-permute-start | bytes 196616 | tf_op jit(solution)/shard_map/ppermute | solution.py:300
  44.3 8.9 %collective-permute-start.4 = (bf16[32,1024]{1,0:T(8,128)(2,1)S(1)}, bf16[32,1024]{1,0:T(8,128)(2,1)S(1)}, u32[]{:S(2)}, u32[]{:S(2)}) collective-permute-start(bf16[32,1024]{1,0:T(8,128)(2,1)S(1)} %get-tuple-element.44), channel_id=1, source_target_pairs={{0,760},{8,16},{16,8},{24,32},{32,24},{40,48},{48,40},{56,64},{64,... | collective-permute-start | bytes 196616 | tf_op jit(solution)/shard_map/ppermute | solution.py:291
  49.2 4.0 %collective-permute-start.5 = (bf16[32,1024]{1,0:T(8,128)(2,1)S(1)}, bf16[32,1024]{1,0:T(8,128)(2,1)S(1)}, u32[]{:S(2)}, u32[]{:S(2)}) collective-permute-start(bf16[32,1024]{1,0:T(8,128)(2,1)S(1)} %get-tuple-element.42), channel_id=1, source_target_pairs={{384,392},{392,384},{400,408},{408,400},{416,424},{424,416},{432,4... | collective-permute-start | bytes 196616 | tf_op jit(solution)/shard_map/ppermute | solution.py:300

commit v2 on v0

--- a/solution.py
+++ b/solution.py
@@ -12,6 +12,7 @@
 FAIR_ALPHA = 0.95
 OBJECTIVE_WEIGHT = 64.0
 ROWS = 112
+SENT = 104
 CHUNK = 512
 
 F32 = jnp.float32
@@ -137,7 +138,7 @@
     forecast = (base_t[...] + (parts[:ROWS] + parts[ROWS:])).astype(BF16)
     mine[...] = forecast
     for m in range(piled.shape[0]):
-        piled[m] = forecast
+        piled[m] = forecast[:SENT]
     slots = keyval.shape[0]
     pad = jnp.zeros((slots, 128 - ROWS), BF16)
     for p in range(PAIRS):
@@ -158,12 +159,19 @@
             value_joint[rows, :] = jnp.concatenate([high, pad, low, pad], 1)
 
 
+def widen(piled, wide):
+    for m in range(piled.shape[0]):
+        wide[m, :SENT] = piled[m].astype(F32)
+        wide[m, SENT:] = jnp.zeros((ROWS - SENT, wide.shape[2]), F32)
+
+
 def backward_kernel(
     info, piled, mine, analysis_t, scale_t, joint_t, query_halves, value_joint, weight, weight_16,
     slant, keyval_weight, keep,
     term_across, term_beside, term_own, grad_score, slope,
-    partial, slope_t, truth, terms, grad_weight,
+    partial, slope_t, truth, terms, grad_weight, wide,
 ):
+    widen(piled, wide)
     members = piled.shape[0]
     fair_eps = (1.0 - FAIR_ALPHA) / members
     variables = analysis_t.shape[0]
@@ -179,7 +187,7 @@
         forecast = mine[at].astype(F32)
         spread = jnp.zeros_like(forecast)
         for k in range(members):
-            spread = spread + bend(forecast - piled[k, at].astype(F32))
+            spread = spread + bend(forecast - wide[k, at])
         slope_t[at] = (OBJECTIVE_WEIGHT * scale_t[at]) * (
             bend(forecast - truth[at]) * (1.0 / members)
             - ((1.0 - fair_eps) / (members * (members - 1))) * spread
@@ -226,8 +234,9 @@
     info, keyval, grad_score, query_weight, slope, channels_t, piled, analysis_t, scale_t,
     term_own, from_beside,
     grad_grid, penalty, total,
-    grad_query, truth, turned,
+    grad_query, truth, turned, wide,
 ):
+    widen(piled, wide)
     total[...] = term_own[...].astype(F32) + from_beside[...].astype(F32)
     variables = channels_t.shape[0]
     for p in range(PAIRS):
@@ -251,7 +260,7 @@
     turned[ROWS:] = jnp.zeros((128 - ROWS, 128), F32)
     for r in range(0, ROWS, 16):
         at = slice(r, r + 16)
-        casts = [piled[m, at].astype(F32) for m in range(members)]
+        casts = [wide[m, at] for m in range(members)]
         goal = truth[at]
         accuracy = jnp.zeros_like(goal)
         spread = jnp.zeros_like(goal)
@@ -387,7 +396,7 @@
     piled, mine, value_joint = call(
         forecast_kernel,
         [
-            shaped(members, ROWS, points),
+            shaped(members, SENT, points),
             shaped(ROWS, points),
             shaped(HEADS * slots, 256),
         ],
@@ -414,6 +423,7 @@
             pltpu.VMEM((ROWS, points), F32),
             pltpu.VMEM((slots, channels), BF16),
             pltpu.VMEM((HEADS * slots, points), F32),
+            pltpu.VMEM((members, ROWS, points), F32),
         ],
         (
             info, piled, mine, analysis_t, scale_t, joint_t, query_halves, value_joint, weight,
@@ -437,6 +447,7 @@
             pltpu.VMEM((points, channels), BF16),
             pltpu.VMEM((ROWS, points), F32),
             pltpu.VMEM((128, 128), F32),
+            pltpu.VMEM((members, ROWS, points), F32),
         ],
         (
             info, keyval, grad_score, query_weight, slope, channels_t, piled, analysis_t, scale_t,

time: 54.3 us -> 54 us (level)
  no operation moved by 1% of the time
where the time goes in v2:
time: 54 us; the launch traced here: 53.7 us
  starting transfers between devices  25.6 us (47%)
  blocking collectives  15.6 us (29%)
  Pallas kernels  9.16 us (17%)
  local copies, waits for them, and re-layouts  1.44 us (3%)
  between operations  0.86 us (2%)
  other arithmetic  0.73 us (1%)
    ppermute x2, starting transfers between devices, swap_across(): lax.ppermute(value, 'space', [(i, (i + 1) % count if i % 2 else (i - 1) %...  20.9 us
    all_to_all x1, blocking collectives, per_device(): lax.all_to_all(piled, 'member', split_axis=0, concat_axis=0, tiled=True)  15.6 us
    pallas_call x7, Pallas kernels, call(): pl.pallas_call(kernel, out_shape=outs, in_specs=specs, out_specs=[VMEM] *...  9.16 us
    ppermute x3, starting transfers between devices, swap_beside(): return lax.ppermute(value, 'space', [(i, i ^ 1) for i in chosen])  4.64 us
    unnamed x22, local copies, waits for them, and re-layouts  1.44 us
  transfers between devices with their start and end apart: 5, of which 1 were waited for; matrix products, arithmetic and copies ran while one was open for 0% of the time, Pallas kernels for 7%

profile of v2, /device:TPU:8, one launch (start us, length us, event | category | flops | bytes accessed | tf_op | source)
XLA Modules:
  0.0 53.7 jit_solution(11453296791496499596)
XLA Ops:
  0.6 0.0 copy-start.7
  0.6 0.0 copy-start.2
  0.7 0.0 copy-start.6
  0.7 2.1 %collective-permute-start.2 = (bf16[32,1024]{1,0:T(8,128)(2,1)}, bf16[32,1024]{1,0:T(8,128)(2,1)S(1)}, u32[]{:S(2)}, u32[]{:S(2)}) collective-permute-start(bf16[32,1024]{1,0:T(8,128)(2,1)} %bitcast.20), channel_id=1, source_target_pairs={{0,8},{8,0},{16,24},{24,16},{32,40},{40,32},{48,56},{56,48},{64,72... | collective-permute-start | bytes 196616 | tf_op jit(solution)/shard_map/ppermute | solution.py:313
  2.7 15.0 %collective-permute-start.1 = (bf16[32,1024]{1,0:T(8,128)(2,1)}, bf16[32,1024]{1,0:T(8,128)(2,1)S(1)}, u32[]{:S(2)}, u32[]{:S(2)}) collective-permute-start(bf16[32,1024]{1,0:T(8,128)(2,1)} %bitcast.21), channel_id=1, source_target_pairs={{0,760},{8,16},{16,8},{24,32},{32,24},{40,48},{48,40},{56,64},{64,... | collective-permute-start | bytes 196616 | tf_op jit(solution)/shard_map/ppermute | solution.py:304
  17.7 0.0 copy-done.7
  17.7 0.7 %collective-permute-start = (bf16[32,1024]{1,0:T(8,128)(2,1)S(1)}, bf16[32,1024]{1,0:T(8,128)(2,1)S(1)}, u32[]{:S(2)}, u32[]{:S(2)}) collective-permute-start(bf16[32,1024]{1,0:T(8,128)(2,1)S(1)} %bitcast.22), channel_id=1, source_target_pairs={{384,392},{392,384},{400,408},{408,400},{416,424},{424,416},{432,4... | collective-permute-start | bytes 196616 | tf_op jit(solution)/shard_map/ppermute | solution.py:313
  18.4 0.0 copy-done.2
  18.4 0.0 copy-done.6
  18.4 0.0 copy-start
  18.4 0.0 copy-start.3
  18.5 0.0 copy-start.5
  18.5 0.0 copy-start.1
  18.5 0.8 %shard_map.133.joint_t = bf16[224,1024]{1,0:T(8,128)(2,1)S(1)} custom-call(bf16[1024,1024]{1,0:T(8,128)(2,1)S(1)} %copy-done.6, bf16[100,1024]{1,0:T(8,128)(2,1)S(1)} %bitcast.13), custom_call_target="tpu_custom_call" | custom-call | flops 3000000000 | bytes 10000000 | tf_op jit(solution)/shard_map/pallas_call | solution.py:291
  19.3 0.0 copy-start.8
  19.3 0.0 copy-start.9
  19.3 0.0 copy-start.10
  19.3 0.7 %copy-done = bf16[1024,1024]{1,0:T(8,128)(2,1)S(1)} copy-done((bf16[1024,1024]{1,0:T(8,128)(2,1)S(1)}, bf16[1024,1024]{1,0:T(8,128)(2,1)}, u32[]{:S(2)}) %copy-start) | copy-done | bytes 2097176
  20.0 0.0 copy-done.3
  20.0 0.0 copy-done.5
  20.0 0.6 %shard_map.131 = (bf16[128,1024]{1,0:T(8,128)(2,1)S(1)}, bf16[1024,128]{1,0:T(8,128)(2,1)S(1)}, bf16[1024,128]{1,0:T(8,128)(2,1)S(1)}, f32[112,128]{1,0:T(8,128)S(1)}) custom-call(bf16[128,1024]{1,0:T(8,128)(2,1)S(1)} %bitcast.16, bf16[1024,1024]{1,0:T(8,128)(2,1)S(1)} %copy-done, bf16[100,1024]{1,0:T(8,128)(2,1)S(1)} %bitcast.14, f32[100,1,128]{2,1,0:T(1,128)S(1)} %bitcast.19), custom_call_target="tpu_custom_call" | custom-call | flops 1000000 | bytes 1000000 | tf_op jit(solution)/shard_map/pallas_call | solution.py:291
  20.6 0.1 pad_add_fusion.info
  20.7 0.0 collective-permute-done.beside_late
  20.7 0.0 collective-permute-done.2.beside_early
  20.7 0.0 collective-permute-done.1.across
  20.7 0.7 %copy-done.1 = bf16[1024,2048]{1,0:T(8,128)(2,1)S(1)} copy-done((bf16[1024,2048]{1,0:T(8,128)(2,1)S(1)}, bf16[1024,2048]{1,0:T(8,128)(2,1)}, u32[]{:S(2)}) %copy-start.1) | copy-done | bytes 4194328
  21.4 0.0 copy-done.8
  21.4 0.0 copy-done.9
  21.4 0.0 copy-done.10
  21.4 2.1 %shard_map.132 = (bf16[96,2048]{1,0:T(8,128)(2,1)S(1)}, f32[8,96,256]{2,1,0:T(8,128)S(1)}, bf16[8,96,256]{2,1,0:T(8,128)(2,1)S(1)}, f32[8,96,256]{2,1,0:T(8,128)...) custom-call(s32[2]{0:T(128)S(1)} %pad_add_fusion.info, ...), custom_call_target="tpu_custom_call" | custom-call | flops 2000000000 | bytes 8000000 | tf_op jit(solution)/shard_map/pallas_call | solution.py:291
  23.5 0.0 copy-start.4
  23.5 0.5 shard_map.134
  24.0 15.6 %all_to_all.5.piled = bf16[8,104,128]{2,1,0:T(8,128)(2,1)S(1)} all-to-all(bf16[8,104,128]{2,1,0:T(8,128)(2,1)S(1)} %get-tuple-element.35), channel_id=1, replica_groups=mesh['space'=96,'member'=8] {'member'}, dimensions={0} | all-to-all | bytes 425984 | tf_op jit(solution)/shard_map/all_to_all | solution.py:410
  39.6 0.0 copy-done.4
  39.6 2.6 %shard_map.135 = (bf16[32,1024]{1,0:T(8,128)(2,1)S(1)}, bf16[32,1024]{1,0:T(8,128)(2,1)S(1)}, bf16[32,1024]{1,0:T(8,128)(2,1)S(1)}, bf16[8,96,256]{2,1,0:T(8,128)(2,1)S(1)}, bf16[128,128]{1,0:T(8,128)(2,1)S(1)}) custom-call(s32[2]{0:T(128)S(1)} %pad_add_fusion.info, bf16[8,104,128]{2,1,0:T(8,128)(2,1)S(1)} %all_to_all.5.piled, ...), custom_call_target="tpu_custom_call" | custom-call | flops 1500000000 | bytes 8000000 | tf_op jit(solution)/shard_map/pallas_call | solution.py:291
  42.3 1.9 %collective-permute-start.3 = (bf16[32,1024]{1,0:T(8,128)(2,1)S(1)}, bf16[32,1024]{1,0:T(8,128)(2,1)S(1)}, u32[]{:S(2)}, u32[]{:S(2)}) collective-permute-start(bf16[32,1024]{1,0:T(8,128)(2,1)S(1)} %get-tuple-element.46), channel_id=1, source_target_pairs={{0,8},{8,0},{16,24},{24,16},{32,40},{40,32},{48,56},{56,48},{64,72... | collective-permute-start | bytes 196616 | tf_op jit(solution)/shard_map/ppermute | solution.py:313
  44.2 6.0 %collective-permute-start.4 = (bf16[32,1024]{1,0:T(8,128)(2,1)S(1)}, bf16[32,1024]{1,0:T(8,128)(2,1)S(1)}, u32[]{:S(2)}, u32[]{:S(2)}) collective-permute-start(bf16[32,1024]{1,0:T(8,128)(2,1)S(1)} %get-tuple-element.48), channel_id=1, source_target_pairs={{0,760},{8,16},{16,8},{24,32},{32,24},{40,48},{48,40},{56,64},{64,... | collective-permute-start | bytes 196616 | tf_op jit(solution)/shard_map/ppermute | solution.py:304
  50.1 0.0 collective-permute-done.3.from_beside
  50.2 2.5 %shard_map.136 = (bf16[128,1024]{1,0:T(8,128)(2,1)}, f32[16,100]{1,0:T(8,128)}, f32[32,1024]{1,0:T(8,128)S(1)}) custom-call(s32[2]{0:T(128)S(1)} %pad_add_fusion.info, bf16[96,2048]{1,0:T(8,128)(2,1)S(1)} %get-tuple-element.32.keyval, bf16[8,96,256]{2,1,0:T(8,128)(2,1)S(1)} %get-tuple-element.43.grad_score, bf16[1024,1024]{1,0:T(8,128)(2,1)S(1)} %copy-done, ...), custom_call_target="tpu_custom_call" | custom-call | flops 400000000 | bytes 4000000 | tf_op jit(solution)/shard_map/pallas_call | solution.py:291
  52.7 0.4 collective-permute-done.4
  53.1 0.7 %fusion = bf16[1,32,1024]{2,1,0:T(8,128)(2,1)} fusion(f32[32,1024]{1,0:T(8,128)S(1)} %get-tuple-element.47, bf16[32,1024]{1,0:T(8,128)(2,1)S(1)} %collective-permute-done.4), kind=kLoop, calls=%fused_computation.1 | loop fusion | flops 98304 | bytes 262144 | tf_op jit(solution)/shard_map/broadcast_in_dim | solution.py:462
  (1 shorter events, 0.0 us)
Async XLA Ops:
  0.6 17.1 %copy-start.7 = (bf16[1,32,1024]{2,1,0:T(8,128)(2,1)S(1)}, bf16[1,32,1024]{2,1,0:T(8,128)(2,1)}, u32[]{:S(2)}) copy-start(bf16[1,32,1024]{2,1,0:T(8,128)(2,1)} %param.11) | copy-start | bytes 196612
  0.6 17.8 %copy-start.2 = (bf16[1024,100]{0,1:T(8,128)(2,1)S(1)}, bf16[1024,100]{0,1:T(8,128)(2,1)}, u32[]{:S(2)}) copy-start(bf16[1024,100]{0,1:T(8,128)(2,1)} %param.21) | copy-start | bytes 614404
  0.7 17.8 %copy-start.6 = (bf16[1024,1024]{1,0:T(8,128)(2,1)S(1)}, bf16[1024,1024]{1,0:T(8,128)(2,1)}, u32[]{:S(2)}) copy-start(bf16[1024,1024]{1,0:T(8,128)(2,1)} %output_weight.1) | copy-start | bytes 6291460
  0.7 20.0 %collective-permute-start.2 = (bf16[32,1024]{1,0:T(8,128)(2,1)}, bf16[32,1024]{1,0:T(8,128)(2,1)S(1)}, u32[]{:S(2)}, u32[]{:S(2)}) collective-permute-start(bf16[32,1024]{1,0:T(8,128)(2,1)} %bitcast.20), channel_id=1, source_target_pairs={{0,8},{8,0},{16,24},{24,16},{32,40},{40,32},{48,56},{56,48},{64,72... | collective-permute-start | bytes 196616 | tf_op jit(solution)/shard_map/ppermute | solution.py:313
  2.7 18.0 %collective-permute-start.1 = (bf16[32,1024]{1,0:T(8,128)(2,1)}, bf16[32,1024]{1,0:T(8,128)(2,1)S(1)}, u32[]{:S(2)}, u32[]{:S(2)}) collective-permute-start(bf16[32,1024]{1,0:T(8,128)(2,1)} %bitcast.21), channel_id=1, source_target_pairs={{0,760},{8,16},{16,8},{24,32},{32,24},{40,48},{48,40},{56,64},{64,... | collective-permute-start | bytes 196616 | tf_op jit(solution)/shard_map/ppermute | solution.py:304
  17.7 3.0 %collective-permute-start = (bf16[32,1024]{1,0:T(8,128)(2,1)S(1)}, bf16[32,1024]{1,0:T(8,128)(2,1)S(1)}, u32[]{:S(2)}, u32[]{:S(2)}) collective-permute-start(bf16[32,1024]{1,0:T(8,128)(2,1)S(1)} %bitcast.22), channel_id=1, source_target_pairs={{384,392},{392,384},{400,408},{408,400},{416,424},{424,416},{432,4... | collective-permute-start | bytes 196616 | tf_op jit(solution)/shard_map/ppermute | solution.py:313
  18.4 1.6 %copy-start = (bf16[1024,1024]{1,0:T(8,128)(2,1)S(1)}, bf16[1024,1024]{1,0:T(8,128)(2,1)}, u32[]{:S(2)}) copy-start(bf16[1024,1024]{1,0:T(8,128)(2,1)} %query_weight.3) | copy-start | bytes 6291460
  18.4 1.6 %copy-start.3 = (bf16[1,128,1024]{2,1,0:T(8,128)(2,1)S(1)}, bf16[1,128,1024]{2,1,0:T(8,128)(2,1)}, u32[]{:S(2)}) copy-start(bf16[1,128,1024]{2,1,0:T(8,128)(2,1)} %param.12) | copy-start | bytes 786436
  18.5 1.6 %copy-start.5 = (f32[1,128,100]{1,0,2:T(1,128)S(1)}, f32[1,128,100]{1,0,2:T(1,128)}, u32[]{:S(2)}) copy-start(f32[1,128,100]{1,0,2:T(1,128)} %param.13) | copy-start | bytes 153604
  18.5 2.9 %copy-start.1 = (bf16[1024,2048]{1,0:T(8,128)(2,1)S(1)}, bf16[1024,2048]{1,0:T(8,128)(2,1)}, u32[]{:S(2)}) copy-start(bf16[1024,2048]{1,0:T(8,128)(2,1)} %keyval_weight.3) | copy-start | bytes 12582916
  19.3 2.1 %copy-start.8 = (s32[128,3]{0,1:T(4,128)S(1)}, s32[128,3]{0,1:T(4,128)}, u32[]{:S(2)}) copy-start(s32[128,3]{0,1:T(4,128)} %param.15) | copy-start | bytes 4612
  19.3 2.1 %copy-start.9 = (f32[128]{0:T(128)S(1)}, f32[128]{0:T(128)}, u32[]{:S(2)}) copy-start(f32[128]{0:T(128)} %param.16) | copy-start | bytes 1540
  19.3 2.1 %copy-start.10 = (f32[100]{0:T(128)S(1)}, f32[100]{0:T(128)}, u32[]{:S(2)}) copy-start(f32[100]{0:T(128)} %param.17) | copy-start | bytes 1204
  23.5 16.1 %copy-start.4 = (f32[128,100]{0,1:T(8,128)S(1)}, f32[128,100]{0,1:T(8,128)}, u32[]{:S(2)}) copy-start(f32[128,100]{0,1:T(8,128)} %param.14) | copy-start | bytes 153604
  42.3 7.9 %collective-permute-start.3 = (bf16[32,1024]{1,0:T(8,128)(2,1)S(1)}, bf16[32,1024]{1,0:T(8,128)(2,1)S(1)}, u32[]{:S(2)}, u32[]{:S(2)}) collective-permute-start(bf16[32,1024]{1,0:T(8,128)(2,1)S(1)} %get-tuple-element.46), channel_id=1, source_target_pairs={{0,8},{8,0},{16,24},{24,16},{32,40},{40,32},{48,56},{56,48},{64,72... | collective-permute-start | bytes 196616 | tf_op jit(solution)/shard_map/ppermute | solution.py:313
  44.2 8.9 %collective-permute-start.4 = (bf16[32,1024]{1,0:T(8,128)(2,1)S(1)}, bf16[32,1024]{1,0:T(8,128)(2,1)S(1)}, u32[]{:S(2)}, u32[]{:S(2)}) collective-permute-start(bf16[32,1024]{1,0:T(8,128)(2,1)S(1)} %get-tuple-element.48), channel_id=1, source_target_pairs={{0,760},{8,16},{16,8},{24,32},{32,24},{40,48},{48,40},{56,64},{64,... | collective-permute-start | bytes 196616 | tf_op jit(solution)/shard_map/ppermute | solution.py:304
